TPU v7x, 512 devices: a whole 4x4x16 slice. The times are simulated.
512 devices in a mesh: dp: 16 (over x_hi, y, core), expert: 32 (over x_lo, z).
Axes of the slice: x: 4 (x_hi: 2, x_lo: 2; x = x_hi * 2 + x_lo), y: 4, z: 16, core: 2. Of those that a mesh axis runs over, the one named last changes fastest.
Arguments:
- tokens: bfloat16 [65536, 1024], P(('dp', 'expert')), may hold values from -6 to 6
- cotangent: bfloat16 [65536, 1024], P(('dp', 'expert')), may hold values from -6 to 6
- picks: int32 [512, 64], P(('dp', 'expert')), may hold values from 0 to 127
- gates: float32 [512, 64], P(('dp', 'expert')), may hold values from 0.1 to 1
- w_gate: bfloat16 [64, 2816, 1024], P('expert', 'dp'), may hold values from -0.1875 to 0.1875
- w_up: bfloat16 [64, 2816, 1024], P('expert', 'dp'), may hold values from -0.1875 to 0.1875
- w_down: bfloat16 [64, 2816, 1024], P('expert', 'dp'), may hold values from -0.109375 to 0.109375
Outputs:
- grad_tokens: bfloat16 [65536, 1024], P(('dp', 'expert'))
- grad_gate: bfloat16 [64, 2816, 1024], P('expert', 'dp')
- grad_up: bfloat16 [64, 2816, 1024], P('expert', 'dp')
- grad_down: bfloat16 [64, 2816, 1024], P('expert', 'dp')
Inputs may be any that keep to these rules, and one draw needn't show every extreme that they name: picks[s, e] is the row, among the 128 tokens of device s, that expert e takes from device s.
All inputs are finite; a program needn't handle non-finite values.
Results may differ from a plain program's by a relative error of at most 0.02.
Values may be sent and summed in bfloat16 or wider, within the bound.
No kernel may reach another device: no remote copies, remote signals or barrier semaphores. Data moves between devices by JAX's collectives and lax.ppermute only.
A program may use at most 64 MiB of HBM per device.

v0:
```python
import jax
import jax.numpy as jnp
from jax import lax
from jax.sharding import PartitionSpec as P


def shards(tokens, cotangent, picks, gates, w_gate, w_up, w_down):
    expert_count = lax.axis_size("expert")
    token_rows, width = tokens.shape
    local_experts = w_gate.shape[0]
    chosen_row = picks[0]
    selector = (chosen_row[:, None] == jnp.arange(token_rows, dtype=jnp.int32)[None, :]).astype(
        jnp.bfloat16
    )
    chosen = jnp.dot(selector, tokens, preferred_element_type=jnp.float32).astype(jnp.bfloat16)
    picked_grad = jnp.dot(selector, cotangent, preferred_element_type=jnp.float32)
    scaled = (picked_grad * gates[0][:, None]).astype(jnp.bfloat16)
    layout = (expert_count, local_experts, width)
    got_x, got_dy = (
        lax.all_to_all(chosen.reshape(layout), "expert", split_axis=0, concat_axis=0, tiled=True),
        lax.all_to_all(scaled.reshape(layout), "expert", split_axis=0, concat_axis=0, tiled=True),
    )
    all_x, all_dy = (
        lax.all_gather(got_x, "dp", axis=0, tiled=True),
        lax.all_gather(got_dy, "dp", axis=0, tiled=True),
    )
    pre_gate = jnp.einsum("sed,efd->esf", all_x, w_gate, preferred_element_type=jnp.float32)
    pre_up = jnp.einsum("sed,efd->esf", all_x, w_up, preferred_element_type=jnp.float32)
    sigmoid_g = jax.nn.sigmoid(pre_gate)
    active = pre_gate * sigmoid_g
    hidden = (active * pre_up).astype(jnp.bfloat16)
    grad_hidden = jnp.einsum("sed,efd->esf", all_dy, w_down, preferred_element_type=jnp.float32)
    grad_down = jnp.einsum(
        "esf,sed->efd", hidden, all_dy, preferred_element_type=jnp.float32
    ).astype(jnp.bfloat16)
    d_up = (grad_hidden * active).astype(jnp.bfloat16)
    d_gate = (grad_hidden * pre_up * sigmoid_g * (1.0 + pre_gate * (1.0 - sigmoid_g))).astype(
        jnp.bfloat16
    )
    grad_gate = jnp.einsum(
        "esf,sed->efd", d_gate, all_x, preferred_element_type=jnp.float32
    ).astype(jnp.bfloat16)
    grad_up = jnp.einsum("esf,sed->efd", d_up, all_x, preferred_element_type=jnp.float32).astype(
        jnp.bfloat16
    )
    first = jnp.einsum("esf,efd->sed", d_gate, w_gate, preferred_element_type=jnp.float32)
    second = jnp.einsum("esf,efd->sed", d_up, w_up, preferred_element_type=jnp.float32)
    summed = lax.psum_scatter(
        (first + second).astype(jnp.bfloat16), "dp", scatter_dimension=0, tiled=True
    ).astype(jnp.float32)
    returned = lax.all_to_all(
        summed.astype(jnp.bfloat16), "expert", split_axis=0, concat_axis=0, tiled=True
    ).astype(summed.dtype)
    back_rows = returned.reshape(expert_count * local_experts, width)
    grad_tokens = jax.ops.segment_sum(back_rows, chosen_row, num_segments=token_rows).astype(
        jnp.bfloat16
    )
    return (grad_tokens, grad_gate, grad_up, grad_down)


def solution(mesh):
    return jax.shard_map(
        shards,
        mesh=mesh,
        in_specs=(
            P(("dp", "expert"), None),
            P(("dp", "expert"), None),
            P(("dp", "expert"), None),
            P(("dp", "expert"), None),
            P("expert", "dp", None),
            P("expert", "dp", None),
            P("expert", "dp", None),
        ),
        out_specs=(
            P(("dp", "expert"), None),
            P("expert", "dp", None),
            P("expert", "dp", None),
            P("expert", "dp", None),
        ),
        check_vma=False,
    )
```

profile of v0, /device:TPU:4, one launch (start us, length us, event | category | flops | bytes accessed | tf_op | source)
XLA Modules:
  0.0 300.1 jit_solution(9503811767197228681)
XLA Ops:
  7.2 0.0 copy-start
  7.2 0.0 all-gather.5.cloned.1.call-start
  7.2 1.2 convolution_convert_fusion.3
  8.5 0.1 reshape.23
  8.5 32.8 %all_to_all.15 = bf16[32,2,1024]{2,1,0:T(2,128)(2,1)S(1)} all-to-all(bf16[32,2,1024]{2,1,0:T(2,128)(2,1)S(1)} %reshape.23), channel_id=1, replica_groups=mesh['dp'=16,'expert'=32] {'expert'}, dimensions={0} | all-to-all | bytes 262144 | tf_op jit(solution)/shard_map/all_to_all | solution.py:20
  41.3 0.7 copy.17
  42.0 0.0 all-gather.5.cloned.1.call-update
  42.0 0.0 all-gather.3.cloned.1.call-start
  42.1 1.2 fusion.1
  43.2 0.1 reshape.22
  43.3 0.0 copy-start.2
  43.3 19.2 %all_to_all.16 = bf16[32,2,1024]{2,1,0:T(2,128)(2,1)S(1)} all-to-all(bf16[32,2,1024]{2,1,0:T(2,128)(2,1)S(1)} %reshape.22), channel_id=1, replica_groups=mesh['dp'=16,'expert'=32] {'expert'}, dimensions={0} | all-to-all | bytes 262144 | tf_op jit(solution)/shard_map/all_to_all | solution.py:21
  62.5 0.7 copy.16
  63.2 0.0 all-gather.3.cloned.1.call-update
  63.2 0.0 reduce-scatter.2.cloned.1.call-start
  63.3 31.0 %all-gather.5.cloned.1.call-done = bf16[512,2,1024]{2,0,1:T(8,128)(2,1)} async-done(((bf16[32,2,1024]{2,0,1:T(8,128)(2,1)}), bf16[512,2,1024]{2,0,1:T(8,128)(2,1)}) %all-gather.5.cloned.1.call-update) | async-done | bytes 2097168 | tf_op jit(solution)/shard_map/all_gather | solution.py:24
  94.3 0.0 copy-done
  94.3 0.0 copy-start.1
  94.3 3.5 %fusion.10 = f32[2,512,176]{1,2,0:T(8,128)} fusion(bf16[512,2,1024]{2,0,1:T(8,128)(2,1)} %all-gather.5.cloned.1.call-done, bf16[2,176,1024]{2,1,0:T(8,128)(2,1)S(1)} %copy-done), kind=kOutput, calls=%fused_computation.21 | convolution fusion | flops 369098752 | bytes 3538944 | tf_op jit(solution)/shard_map/sed,efd->esf/dot_general | solution.py:27
  97.7 0.0 copy-done.2
  97.7 0.0 copy-done.1
  97.7 1.7 fusion.9
  99.4 60.6 %all-gather.3.cloned.1.call-done = bf16[512,2,1024]{2,0,1:T(8,128)(2,1)} async-done(((bf16[32,2,1024]{2,0,1:T(8,128)(2,1)}), bf16[512,2,1024]{2,0,1:T(8,128)(2,1)}) %all-gather.3.cloned.1.call-update) | async-done | bytes 2097168 | tf_op jit(solution)/shard_map/all_gather | solution.py:25
  160.0 3.1 %multiply_convert_fusion.1 = (bf16[2,512,176]{1,2,0:T(8,128)(2,1)S(1)}, bf16[2,512,176]{1,2,0:T(8,128)(2,1)S(1)}) fusion(f32[2,512,176]{1,2,0:T(8,128)} %fusion.10, f32[2,512,176]{1,2,0:T(8,128)} %fusion.9, bf16[512,2,1024]{2,0,1:T(8,128)(2,1)} %all-gather.3.cloned.1.call-done, bf16[2,176,1024]{2,1,0:T(8,128)(2,1)} %param.13), kind=kOutput, calls=%fused_computation.10 | convolution fusion | flops 371441664 | bytes 4980736 | tf_op jit(solution)/shard_map/sed,efd->esf/dot_general | solution.py:32
  163.2 0.0 copy-start.5
  163.2 0.0 copy-start.3
  163.2 0.8 fusion.11
  164.0 0.0 copy-done.5
  164.0 0.1 copy-done.3
  164.1 2.1 fusion
  166.2 0.0 copy-start.4
  166.2 0.0 reduce-scatter.2.cloned.1.call-update
  166.2 1.0 copy-done.4
  167.2 0.0 copy-start.6
  167.2 1.4 convolution_convert_fusion.1
  168.6 92.5 %reduce-scatter.2.cloned.1.call-done = bf16[32,2,1024]{2,0,1:T(8,128)(2,1)} async-done(((bf16[512,2,1024]{2,0,1:T(8,128)(2,1)}), bf16[32,2,1024]{2,0,1:T(8,128)(2,1)}) %reduce-scatter.2.cloned.1.call-update) | async-done | bytes 131088 | tf_op jit(solution)/shard_map/reduce_scatter | solution.py:48
  261.0 1.7 copy.18
  262.7 13.2 %all-to-all-start.2 = ((bf16[32,2,1024]{2,1,0:T(2,128)(2,1)}), bf16[32,2,1024]{2,1,0:T(2,128)(2,1)S(1)}, u32[]{:S(2)}, u32[]{:S(2)}) async-start(bf16[32,2,1024]{2,1,0:T(2,128)(2,1)} %copy.18), calls=%async_computation.3 | async-start | bytes 262144 | tf_op jit(solution)/shard_map/all_to_all | solution.py:51
  275.9 0.0 copy-done.6
  275.9 0.0 copy-start.7
  275.9 0.0 copy-start.8
  276.0 1.4 convolution_convert_fusion.2
  277.4 0.0 copy-done.7
  277.4 0.0 copy-done.8
  277.4 3.1 %convolution_convert_fusion = bf16[2,176,1024]{2,1,0:T(8,128)(2,1)} fusion(bf16[512,2,1024]{2,0,1:T(8,128)(2,1)} %all-gather.3.cloned.1.call-done, f32[2,512,176]{1,2,0:T(8,128)S(1)} %copy-done.8, f32[2,512,176]{1,2,0:T(8,128)S(1)} %copy-done.7), kind=kOutput, calls=%fused_computation.3 | convolution fusion | flops 370540544 | bytes 4259840 | tf_op jit(solution)/shard_map/esf,sed->efd/dot_general | solution.py:33
  280.4 11.0 %all-to-all-done.2 = bf16[32,2,1024]{2,1,0:T(2,128)(2,1)S(1)} async-done(((bf16[32,2,1024]{2,1,0:T(2,128)(2,1)}), bf16[32,2,1024]{2,1,0:T(2,128)(2,1)S(1)}, u32[]{:S(2)}, u32[]{:S(2)}) %all-to-all-start.2) | async-done | bytes 131104 | tf_op jit(solution)/shard_map/all_to_all | solution.py:51
  291.5 1.3 scatter_custom_fusion
  292.8 0.7 convert_element_type.43
  (1 shorter events, 0.0 us)
Async XLA Ops:
  7.2 87.1 %copy-start = (bf16[2,176,1024]{2,1,0:T(8,128)(2,1)S(1)}, bf16[2,176,1024]{2,1,0:T(8,128)(2,1)}, u32[]{:S(2)}) copy-start(bf16[2,176,1024]{2,1,0:T(8,128)(2,1)} %param.11) | copy-start | bytes 2162692
  7.2 87.1 %all-gather.5.cloned.1.call-start = ((), (), s32[]{:S(2)}) async-start(), calls=%async_computation.5 | async-start | bytes 2228224 | tf_op jit(solution)/shard_map/all_gather | solution.py:24
  42.0 118.0 %all-gather.3.cloned.1.call-start = ((), (), s32[]{:S(2)}) async-start(), calls=%async_computation.4 | async-start | bytes 2228224 | tf_op jit(solution)/shard_map/all_gather | solution.py:25
  43.3 54.4 %copy-start.2 = (bf16[2,176,1024]{2,1,0:T(8,128)(2,1)S(1)}, bf16[2,176,1024]{2,1,0:T(8,128)(2,1)}, u32[]{:S(2)}) copy-start(bf16[2,176,1024]{2,1,0:T(8,128)(2,1)} %param.12) | copy-start | bytes 2162692
  63.2 197.8 %reduce-scatter.2.cloned.1.call-start = ((), (), s32[]{:S(2)}) async-start(), calls=%async_computation.6 | async-start | bytes 2228224 | tf_op jit(solution)/shard_map/reduce_scatter | solution.py:48
  94.3 3.5 %copy-start.1 = (bf16[512,2,1024]{2,0,1:T(8,128)(2,1)S(1)}, bf16[512,2,1024]{2,0,1:T(8,128)(2,1)}, u32[]{:S(2)}) copy-start(bf16[512,2,1024]{2,0,1:T(8,128)(2,1)} %all-gather.5.cloned.1.call-done) | copy-start | bytes 6291460
  163.2 0.8 copy-start.5
  163.2 0.8 copy-start.3
  166.2 1.0 copy-start.4
  167.2 108.8 %copy-start.6 = (bf16[2,512,176]{1,2,0:T(8,128)(2,1)S(1)}, bf16[2,512,176]{1,2,0:T(8,128)(2,1)}, u32[]{:S(2)}) copy-start(bf16[2,512,176]{1,2,0:T(8,128)(2,1)} %copy-done.5) | copy-start | bytes 1081348
  262.7 28.7 %all-to-all-start.2 = ((bf16[32,2,1024]{2,1,0:T(2,128)(2,1)}), bf16[32,2,1024]{2,1,0:T(2,128)(2,1)S(1)}, u32[]{:S(2)}, u32[]{:S(2)}) async-start(bf16[32,2,1024]{2,1,0:T(2,128)(2,1)} %copy.18), calls=%async_computation.3 | async-start | bytes 262144 | tf_op jit(solution)/shard_map/all_to_all | solution.py:51
  275.9 1.4 copy-start.7
  275.9 1.4 copy-start.8
Sparse Core Ops, SparseCore 0:
  42.1 52.0 all-gather.4
  98.2 61.7 all-gather.2
  166.3 94.6 reduce-scatter.1
where the time goes:
time: 300 us
  waiting for transfers between devices  195 us (65%)
  blocking collectives  52 us (17%)
  matrix products  19.5 us (6%)
  between operations  13.9 us (5%)
  starting transfers between devices  13.3 us (4%)
  local copies, waits for them, and re-layouts  4.26 us (1%)
    reduce_scatter x1, waiting for transfers between devices, shards(): lax.psum_scatter((first + second).astype(jnp.bfloat16), 'dp', scatter_dim...  92.5 us
    all_gather x1, waiting for transfers between devices, shards(): lax.all_gather(got_dy, 'dp', axis=0, tiled=True)  60.6 us
    all_to_all x1, blocking collectives, shards(): lax.all_to_all(chosen.reshape(layout), 'expert', split_axis=0, concat_axi...  32.8 us
    all_gather x1, waiting for transfers between devices, shards(): lax.all_gather(got_x, 'dp', axis=0, tiled=True)  31 us
    all_to_all x1, blocking collectives, shards(): lax.all_to_all(scaled.reshape(layout), 'expert', split_axis=0, concat_axi...  19.2 us
    all_to_all x1, starting transfers between devices, shards(): lax.all_to_all(summed.astype(jnp.bfloat16), 'expert', split_axis=0, conca...  13.2 us
    all_to_all x1, waiting for transfers between devices, shards(): lax.all_to_all(summed.astype(jnp.bfloat16), 'expert', split_axis=0, conca...  11 us
  transfers between devices with their start and end apart: 4, of which 4 were waited for; matrix products, arithmetic and copies ran while one was open for 4% of the time, Pallas kernels for 0%

commit v1 on v0

--- a/solution.py
+++ b/solution.py
@@ -22,7 +22,9 @@
     )
     all_x, all_dy = (
         lax.all_gather(got_x, "dp", axis=0, tiled=True),
-        lax.all_gather(got_dy, "dp", axis=0, tiled=True),
+        jnp.concatenate(
+            lax.all_to_all(jnp.stack([got_dy] * lax.axis_size("dp")), "dp", 0, 0), axis=0
+        ),
     )
     pre_gate = jnp.einsum("sed,efd->esf", all_x, w_gate, preferred_element_type=jnp.float32)
     pre_up = jnp.einsum("sed,efd->esf", all_x, w_up, preferred_element_type=jnp.float32)

time: 300 us -> 241 us (0.80)
  waiting for transfers between devices: 195 us -> 97.1 us
  blocking collectives: 52 us -> 91 us
  matrix products: 19.5 us -> 15.2 us
  local copies, waits for them, and re-layouts: 4.26 us -> 7.3 us
    all_gather x1 -> x0, waiting for transfers between devices: 60.6 us -> none  [shards(): lax.all_gather(got_dy, 'dp', axis=0, tiled=True)]
    all_to_all x0 -> x1, blocking collectives: none -> 39.2 us  [shards(): lax.all_to_all(jnp.stack([got_dy] * lax.axis_size('dp')), 'dp', 0, 0)]
    all_gather x1, waiting for transfers between devices: 31 us -> 0.01 us  [shards(): lax.all_gather(got_x, 'dp', axis=0, tiled=True)]
    reduce_scatter x1, waiting for transfers between devices: 92.5 us -> 86.2 us  [shards(): lax.psum_scatter((first + second).astype(jnp.bfloat16), 'dp', scatter_dim...]
  transfers between devices with their start and end apart: 4 -> 3, of which waited for: 4 -> 2; matrix products, arithmetic and copies ran while one was open for 4% -> 4% of each run, Pallas kernels for 0% -> 0%
where the time goes in v1:
time: 241 us; the launch traced here: 240 us
  waiting for transfers between devices  97.1 us (40%)
  blocking collectives  91 us (38%)
  matrix products  15.2 us (6%)
  between operations  14.2 us (6%)
  starting transfers between devices  13.3 us (6%)
  local copies, waits for them, and re-layouts  7.3 us (3%)
    reduce_scatter x1, waiting for transfers between devices, shards(): lax.psum_scatter((first + second).astype(jnp.bfloat16), 'dp', scatter_dim...  86.2 us
    all_to_all x1, blocking collectives, shards(): lax.all_to_all(jnp.stack([got_dy] * lax.axis_size('dp')), 'dp', 0, 0)  39.2 us
    all_to_all x1, blocking collectives, shards(): lax.all_to_all(chosen.reshape(layout), 'expert', split_axis=0, concat_axi...  32.8 us
    all_to_all x1, blocking collectives, shards(): lax.all_to_all(scaled.reshape(layout), 'expert', split_axis=0, concat_axi...  19.1 us
    all_to_all x1, starting transfers between devices, shards(): lax.all_to_all(summed.astype(jnp.bfloat16), 'expert', split_axis=0, conca...  13.2 us
    all_to_all x1, waiting for transfers between devices, shards(): lax.all_to_all(summed.astype(jnp.bfloat16), 'expert', split_axis=0, conca...  10.9 us
  transfers between devices with their start and end apart: 3, of which 2 were waited for; matrix products, arithmetic and copies ran while one was open for 4% of the time, Pallas kernels for 0%

profile of v1, /device:TPU:4, one launch (start us, length us, event | category | flops | bytes accessed | tf_op | source)
XLA Modules:
  0.0 240.3 jit_solution(15167621988703329014)
XLA Ops:
  7.2 0.0 copy-start
  7.2 0.0 all-gather.2.cloned.1.call-start
  7.2 1.2 convolution_convert_fusion.3
  8.5 0.1 reshape.29
  8.5 32.8 %all_to_all.20 = bf16[32,2,1024]{2,1,0:T(2,128)(2,1)S(1)} all-to-all(bf16[32,2,1024]{2,1,0:T(2,128)(2,1)S(1)} %reshape.29), channel_id=1, replica_groups=mesh['dp'=16,'expert'=32] {'expert'}, dimensions={0} | all-to-all | bytes 262144 | tf_op jit(solution)/shard_map/all_to_all | solution.py:20
  41.3 0.7 copy.18
  42.0 0.0 all-gather.2.cloned.1.call-update
  42.0 0.0 reduce-scatter.2.cloned.1.call-start
  42.1 1.2 fusion.1
  43.2 0.1 reshape.27
  43.3 19.1 %all_to_all.21 = bf16[32,2,1024]{2,1,0:T(2,128)(2,1)S(1)} all-to-all(bf16[32,2,1024]{2,1,0:T(2,128)(2,1)S(1)} %reshape.27), channel_id=1, replica_groups=mesh['dp'=16,'expert'=32] {'expert'}, dimensions={0} | all-to-all | bytes 262144 | tf_op jit(solution)/shard_map/all_to_all | solution.py:21
  62.4 0.2 stack.2
  62.7 39.2 %all_to_all.22 = bf16[16,32,2,1024]{3,1,2,0:T(8,128)(2,1)S(1)} all-to-all(bf16[16,32,2,1024]{3,1,2,0:T(8,128)(2,1)S(1)} %stack.2), channel_id=1, replica_groups=mesh['dp'=16,'expert'=32] {'dp'}, dimensions={0} | all-to-all | bytes 4194304 | tf_op jit(solution)/shard_map/all_to_all | solution.py:26
  101.9 1.5 copy.17
  103.4 0.0 copy-start.2
  103.4 0.0 all-gather.2.cloned.1.call-done
  103.4 0.0 copy-done
  103.4 0.0 copy-start.1
  103.4 2.6 %fusion.10 = f32[2,512,176]{1,2,0:T(8,128)S(1)} fusion(bf16[512,2,1024]{2,0,1:T(8,128)(2,1)} %all-gather.2.cloned.1.call-done, bf16[2,176,1024]{2,1,0:T(8,128)(2,1)S(1)} %copy-done), kind=kOutput, calls=%fused_computation.21 | convolution fusion | flops 369098752 | bytes 3538944 | tf_op jit(solution)/shard_map/sed,efd->esf/dot_general | solution.py:29
  106.0 0.0 copy-done.2
  106.0 0.0 copy-done.1
  106.0 0.0 copy-start.9
  106.0 0.0 copy-start.3
  106.0 0.0 copy-start.12
  106.0 0.8 fusion.9
  106.9 0.0 copy-start.11
  106.9 1.0 copy-done.3
  107.9 0.4 copy-done.12
  108.3 1.0 multiply_convert_fusion.1
  109.3 0.0 copy-done.9
  109.3 0.0 copy-done.11
  109.3 0.0 copy-start.7
  109.3 0.0 copy-start.5
  109.3 0.8 fusion.11
  110.1 0.0 copy-done.7
  110.1 0.1 copy-done.5
  110.2 2.1 fusion
  112.3 0.0 copy-start.6
  112.3 0.0 reduce-scatter.2.cloned.1.call-update
  112.3 1.0 copy-done.6
  113.3 0.0 copy-start.8
  113.3 1.4 convolution_convert_fusion.1
  114.7 86.2 %reduce-scatter.2.cloned.1.call-done = bf16[32,2,1024]{2,0,1:T(8,128)(2,1)} async-done(((bf16[512,2,1024]{2,0,1:T(8,128)(2,1)}), bf16[32,2,1024]{2,0,1:T(8,128)(2,1)}) %reduce-scatter.2.cloned.1.call-update) | async-done | bytes 131088 | tf_op jit(solution)/shard_map/reduce_scatter | solution.py:50
  200.9 1.7 copy.19
  202.6 13.2 %all-to-all-start.3 = ((bf16[32,2,1024]{2,1,0:T(2,128)(2,1)}), bf16[32,2,1024]{2,1,0:T(2,128)(2,1)S(1)}, u32[]{:S(2)}, u32[]{:S(2)}) async-start(bf16[32,2,1024]{2,1,0:T(2,128)(2,1)} %copy.19), calls=%async_computation.4 | async-start | bytes 262144 | tf_op jit(solution)/shard_map/all_to_all | solution.py:53
  215.8 0.0 copy-done.8
  215.8 0.0 copy-start.4
  215.8 0.0 copy-start.10
  215.8 1.4 convolution_convert_fusion.2
  217.2 0.3 copy-done.4
  217.5 0.3 copy-done.10
  217.8 2.6 %convolution_convert_fusion = bf16[2,176,1024]{2,1,0:T(8,128)(2,1)} fusion(bf16[512,2,1024]{2,0,1:T(8,128)(2,1)S(1)} %bitcast.23, f32[2,512,176]{1,2,0:T(8,128)} %copy-done.11, f32[2,512,176]{1,2,0:T(8,128)S(1)} %copy-done.10), kind=kOutput, calls=%fused_computation.3 | convolution fusion | flops 370540544 | bytes 4259840 | tf_op jit(solution)/shard_map/esf,sed->efd/dot_general | solution.py:35
  220.4 10.9 %all-to-all-done.3 = bf16[32,2,1024]{2,1,0:T(2,128)(2,1)S(1)} async-done(((bf16[32,2,1024]{2,1,0:T(2,128)(2,1)}), bf16[32,2,1024]{2,1,0:T(2,128)(2,1)S(1)}, u32[]{:S(2)}, u32[]{:S(2)}) %all-to-all-start.3) | async-done | bytes 131104 | tf_op jit(solution)/shard_map/all_to_all | solution.py:53
  231.3 1.3 scatter_custom_fusion
  232.7 0.7 convert_element_type.43
  (2 shorter events, 0.1 us)
Async XLA Ops:
  7.2 96.2 %copy-start = (bf16[2,176,1024]{2,1,0:T(8,128)(2,1)S(1)}, bf16[2,176,1024]{2,1,0:T(8,128)(2,1)}, u32[]{:S(2)}) copy-start(bf16[2,176,1024]{2,1,0:T(8,128)(2,1)} %param.11) | copy-start | bytes 2162692
  7.2 96.2 %all-gather.2.cloned.1.call-start = ((), (), s32[]{:S(2)}) async-start(), calls=%async_computation.5 | async-start | bytes 2228224 | tf_op jit(solution)/shard_map/all_gather | solution.py:24
  42.0 158.9 %reduce-scatter.2.cloned.1.call-start = ((), (), s32[]{:S(2)}) async-start(), calls=%async_computation.6 | async-start | bytes 2228224 | tf_op jit(solution)/shard_map/reduce_scatter | solution.py:50
  103.4 2.6 %copy-start.2 = (bf16[2,176,1024]{2,1,0:T(8,128)(2,1)S(1)}, bf16[2,176,1024]{2,1,0:T(8,128)(2,1)}, u32[]{:S(2)}) copy-start(bf16[2,176,1024]{2,1,0:T(8,128)(2,1)} %param.12) | copy-start | bytes 2162692
  103.4 2.6 %copy-start.1 = (bf16[512,2,1024]{2,0,1:T(8,128)(2,1)S(1)}, bf16[512,2,1024]{2,0,1:T(8,128)(2,1)}, u32[]{:S(2)}) copy-start(bf16[512,2,1024]{2,0,1:T(8,128)(2,1)} %all-gather.2.cloned.1.call-done) | copy-start | bytes 6291460
  106.0 3.3 %copy-start.9 = (f32[2,512,176]{1,2,0:T(8,128)}, f32[2,512,176]{1,2,0:T(8,128)S(1)}, u32[]{:S(2)}) copy-start(f32[2,512,176]{1,2,0:T(8,128)S(1)} %fusion.10) | copy-start | bytes 2162692
  106.0 1.9 copy-start.3
  106.0 2.3 copy-start.12
  106.9 2.4 %copy-start.11 = (f32[2,512,176]{1,2,0:T(8,128)}, f32[2,512,176]{1,2,0:T(8,128)S(1)}, u32[]{:S(2)}) copy-start(f32[2,512,176]{1,2,0:T(8,128)S(1)} %fusion.9) | copy-start | bytes 2162692
  109.3 0.8 copy-start.7
  109.3 0.8 copy-start.5
  112.3 1.0 copy-start.6
  113.3 102.5 %copy-start.8 = (bf16[2,512,176]{1,2,0:T(8,128)(2,1)S(1)}, bf16[2,512,176]{1,2,0:T(8,128)(2,1)}, u32[]{:S(2)}) copy-start(bf16[2,512,176]{1,2,0:T(8,128)(2,1)} %copy-done.7) | copy-start | bytes 1081348
  202.6 28.7 %all-to-all-start.3 = ((bf16[32,2,1024]{2,1,0:T(2,128)(2,1)}), bf16[32,2,1024]{2,1,0:T(2,128)(2,1)S(1)}, u32[]{:S(2)}, u32[]{:S(2)}) async-start(bf16[32,2,1024]{2,1,0:T(2,128)(2,1)} %copy.19), calls=%async_computation.4 | async-start | bytes 262144 | tf_op jit(solution)/shard_map/all_to_all | solution.py:53
  215.8 1.7 copy-start.4
  215.8 2.0 copy-start.10
Sparse Core Ops, SparseCore 0:
  42.1 60.2 all-gather.1
  112.5 88.4 reduce-scatter.1
